TPU v7x, 256 devices: a whole 4x4x8 slice. The times are simulated.
256 devices in a mesh: dom: 128 (over z, y, x), sub: 2 (over core).
Axes of the slice: x: 4, y: 4, z: 8, core: 2. Of those that a mesh axis runs over, the one named last changes fastest.
Arguments:
- pt_old: float32 [26624, 6, 128], P(('dom', 'sub')), may hold values from -6 to 6
- agg_index: int32 [26624], P(('dom', 'sub')), may hold values from 0 to 16383, as said below
- counts: int32 [256], P(('dom', 'sub')), may hold values from 24 to 104
- tiles_a: bfloat16 [16384, 4, 128, 128], P(('dom', 'sub')), may hold values from -0.5 to 0.5
- tile_cols: int32 [16384, 4], P(('dom', 'sub')), may hold values from 0 to 16383, as said below
- inv_diag: float32 [16384, 128], P(('dom', 'sub')), may hold values from 0.25 to 1
Outputs:
- smoothed: float32 [16384, 4, 6, 128], P(('dom', 'sub'))
Inputs may be any that keep to these rules, and one draw needn't show every extreme that they name: `agg_index`: the live slots of all devices name every tile row once. Slots at or beyond the count hold arbitrary numbers. At most 2 live slots of one device name tile rows of one partition (tile row t belongs to partition t // 128). `tile_cols`: slot 0 of tile row t is t itself; every other tile column lies within 16 of t.
All inputs are finite; a program needn't handle non-finite values.
Results may differ from a plain program's by a relative error of at most 0.0018.
Values may be sent and summed in bfloat16 or wider, within the bound.
No kernel may reach another device: no remote copies, remote signals or barrier semaphores. Data moves between devices by JAX's collectives and lax.ppermute only.
A program may use at most 64 MiB of HBM per device.

v0:
```python
import jax
import jax.numpy as jnp
from jax import lax
from jax.sharding import PartitionSpec as P

DAMPING = 2.0 / 3.0


def from_partner(value, axis, stride):
    return lax.ppermute(value, axis, [(i, i ^ 1 << stride) for i in range(lax.axis_size(axis))])


def passed_along(value, axis, steps):
    count = lax.axis_size(axis)
    initial, last = (max(0, -steps), min(count, count - steps))
    return lax.ppermute(value, axis, [(source, source + steps) for source in range(initial, last)])


def per_device(pt_old, agg_index, counts, tiles_a, tile_cols, inv_diag):
    n_dom = lax.axis_size("dom")
    n_sub = lax.axis_size("sub")
    slot_count = pt_old.shape[0]
    modes = pt_old.shape[1]
    width = pt_old.shape[2]
    rows_dev = tiles_a.shape[0]
    part_rows = rows_dev * n_sub
    halo_rows = rows_dev // 4
    most = (slot_count + n_dom - 1) // n_dom + 1
    sub_index = lax.axis_index("sub")
    device = lax.axis_index("dom") * n_sub + sub_index
    slot_ids = jnp.arange(slot_count, dtype=jnp.int32)
    live = slot_ids < counts[0]
    owner = agg_index // part_rows
    earlier = (
        (owner[:, None] == owner[None, :]) & live[None, :] & (slot_ids[None, :] < slot_ids[:, None])
    )
    rank = jnp.sum(earlier.astype(jnp.int32), axis=1)
    target = jnp.where(live, owner * most + rank, n_dom * most)
    outgoing = jnp.zeros((n_dom * most + 1, modes, width), jnp.float32).at[target].set(pt_old)[:-1]
    position = agg_index % part_rows
    send_pos = jnp.full((n_dom * most + 1,), part_rows, jnp.int32).at[target].set(position)[:-1]
    received, arrived = (
        lax.all_to_all(
            outgoing.reshape(n_dom, most, modes, width),
            "dom",
            split_axis=0,
            concat_axis=0,
            tiled=True,
        ),
        lax.all_to_all(
            send_pos.reshape(n_dom, most), "dom", split_axis=0, concat_axis=0, tiled=True
        ),
    )
    received = received.reshape(n_dom * most, modes, width)
    arrived = arrived.reshape(n_dom * most)
    peer_rows, peer_pos = from_partner((received, arrived), "sub", 0)
    both_rows = jnp.concatenate([received, peer_rows], axis=0)
    both_pos = jnp.concatenate([arrived, peer_pos], axis=0) - sub_index * rows_dev
    local = jnp.where((both_pos >= 0) & (both_pos < rows_dev), both_pos, rows_dev)
    pt_here = (
        jnp.zeros((rows_dev + 1, modes, width), jnp.float32).at[local].set(both_rows)[:rows_dev]
    )
    rounded_here = pt_here.astype(jnp.bfloat16)
    below = passed_along(rounded_here[rows_dev - halo_rows :], ("dom", "sub"), 1)
    above = passed_along(rounded_here[:halo_rows], ("dom", "sub"), -1)
    extended = jnp.concatenate([below, rounded_here, above], axis=0)
    local_cols = tile_cols - (device * rows_dev - halo_rows)
    gathered = extended[local_cols]
    product = jnp.einsum("tkcj,tkij->tkci", gathered, tiles_a, preferred_element_type=jnp.float32)
    smooth = -DAMPING * inv_diag[:, None, None, :] * product
    return smooth.at[:, 0].add(pt_here)


def solution(mesh):
    in_specs = (
        P(("dom", "sub"), None, None),
        P(("dom", "sub")),
        P(("dom", "sub")),
        P(("dom", "sub"), None, None, None),
        P(("dom", "sub"), None),
        P(("dom", "sub"), None),
    )
    out_specs = P(("dom", "sub"), None, None, None)
    return jax.shard_map(
        per_device, mesh=mesh, in_specs=in_specs, out_specs=out_specs, check_vma=False
    )
```

profile of v0, /device:TPU:32, one launch (start us, length us, event | category | flops | bytes accessed | tf_op | source)
XLA Modules:
  0.0 105.2 jit_solution(11852337662900893193)
XLA Ops:
  0.0 0.7 and_select_fusion.1
  1.3 1.1 %copy.20 = f32[104,6,128]{2,1,0:T(8,128)S(1)} copy(f32[104,6,128]{2,0,1:T(8,128)} %param.8) | data formatting | bytes 638976 | tf_op args[0]
  2.4 0.2 convert_reduce_fusion
  2.6 0.1 broadcast_in_dim.33
  2.7 4.0 %scatter_fusion = f32[257,6,128]{2,1,0:T(8,128)S(1)} fusion(f32[257,6,128]{2,1,0:T(8,128)S(1)} %broadcast_in_dim.33, s32[104]{0:T(128)S(1)} %compare_select_fusion.2, f32[104,6,128]{2,1,0:T(8,128)S(1)} %copy.20), kind=kCustom, calls=%fused_computation.2 | custom fusion | bytes 958880 | tf_op jit(solution)/shard_map/scatter | solution.py:39
  6.6 0.1 slice.50
  6.7 0.4 copy.21
  7.1 40.7 %all_to_all.14 = f32[128,2,6,128]{3,1,2,0:T(2,128)S(1)} all-to-all(f32[128,2,6,128]{3,1,2,0:T(2,128)S(1)} %copy.21), channel_id=1, replica_groups=mesh['dom'=128,'sub'=2] {'dom'}, dimensions={0} | all-to-all | bytes 1572864 | tf_op jit(solution)/shard_map/all_to_all | solution.py:43
  47.8 0.1 copy.22
  47.9 0.2 copy.23
  48.1 0.1 collective-permute-start.1
  48.2 0.9 scatter_custom_fusion
  49.1 0.8 all_to_all.9
  49.9 6.4 %all-to-all-start = ((s32[128,1,2]{2,1,0:T(1,128)}), s32[128,1,2]{2,1,0:T(1,128)S(1)}, u32[]{:S(2)}, u32[]{:S(2)}) async-start(s32[128,1,2]{2,1,0:T(1,128)} %bitcast.1), calls=%async_computation | async-start | bytes 131072 | tf_op jit(solution)/shard_map/all_to_all | solution.py:50
  56.3 11.5 %all-to-all-done = s32[128,1,2]{2,1,0:T(1,128)S(1)} async-done(((s32[128,1,2]{2,1,0:T(1,128)}), s32[128,1,2]{2,1,0:T(1,128)S(1)}, u32[]{:S(2)}, u32[]{:S(2)}) %all-to-all-start) | async-done | bytes 1056 | tf_op jit(solution)/shard_map/all_to_all | solution.py:50
  67.8 0.1 reshape.111
  67.9 0.1 collective-permute-start
  68.0 0.1 copy.25
  68.1 0.1 reshape.117
  68.2 0.5 broadcast.124
  68.8 0.8 reduce.7
  69.6 0.1 concatenate.22
  69.8 0.5 copy.24
  70.2 0.2 pad_maximum_fusion
  70.5 14.6 %scatter_fusion.1 = f32[65,6,128]{2,1,0:T(8,128)S(1)} fusion(f32[65,6,128]{2,1,0:T(8,128)S(1)} %broadcast_in_dim.16, s32[512]{0:T(512)S(1)} %bitcast.19, f32[512,6,128]{2,1,0:T(8,128)S(1)} %pad_maximum_fusion), kind=kCustom, calls=%fused_computation.3 | custom fusion | bytes 4720640 | tf_op jit(solution)/shard_map/scatter | solution.py:61
  85.1 2.4 %collective-permute-start.2 = (bf16[16,6,128]{2,1,0:T(8,128)(2,1)S(1)}, bf16[16,6,128]{2,1,0:T(8,128)(2,1)S(1)}, u32[]{:S(2)}, u32[]{:S(2)}) collective-permute-start(bf16[16,6,128]{2,1,0:T(8,128)(2,1)S(1)} %get-tuple-element.17), channel_id=1, source_target_pairs={{0,1},{1,2},{2,3},{3,4},{4,5},{5,6},{6,7},{7,8},{8,9},{9,10},{10,1... | collective-permute-start | bytes 73736 | tf_op jit(solution)/shard_map/ppermute | solution.py:16
  87.5 7.4 %collective-permute-start.3 = (bf16[16,6,128]{2,1,0:T(8,128)(2,1)S(1)}, bf16[16,6,128]{2,1,0:T(8,128)(2,1)S(1)}, u32[]{:S(2)}, u32[]{:S(2)}) collective-permute-start(bf16[16,6,128]{2,1,0:T(8,128)(2,1)S(1)} %get-tuple-element.18), channel_id=1, source_target_pairs={{1,0},{2,1},{3,2},{4,3},{5,4},{6,5},{7,6},{8,7},{9,8},{10,9},{11,1... | collective-permute-start | bytes 73736 | tf_op jit(solution)/shard_map/ppermute | solution.py:16
  94.9 1.6 %collective-permute-done.3 = bf16[16,6,128]{2,1,0:T(8,128)(2,1)S(1)} collective-permute-done((bf16[16,6,128]{2,1,0:T(8,128)(2,1)S(1)}, bf16[16,6,128]{2,1,0:T(8,128)(2,1)S(1)}, u32[]{:S(2)}, u32[]{:S(2)}) %collective-permute-start.3) | collective-permute-done | bytes 24608 | tf_op jit(solution)/shard_map/ppermute | solution.py:16
  96.5 0.8 gather_fusion
  97.4 6.7 %convolution_multiply_fusion = f32[64,4,6,128]{3,2,1,0:T(8,128)S(1)} fusion(bf16[64,4,6,128]{3,2,1,0:T(8,128)(2,1)S(1)} %bitcast.17, bf16[64,4,128,128]{3,2,1,0:T(8,128)(2,1)} %param.11, f32[64,128]{1,0:T(8,128)S(1)} %broadcast_multiply_fusion), kind=kOutput, calls=%fused_computation.5 | convolution fusion | flops 50528256 | bytes 9601024 | tf_op jit(solution)/shard_map/tkcj,tkij->tkci/dot_general | solution.py:69
  104.1 0.1 fusion
  104.2 1.1 %copy.26 = f32[64,4,6,128]{3,1,2,0:T(4,128)} copy(f32[64,4,6,128]{3,2,1,0:T(8,128)S(1)} %fusion) | data formatting | bytes 1572864 | tf_op jit(solution)/shard_map/scatter-add | solution.py:71
  (18 shorter events, 0.2 us)
Async XLA Ops:
  47.8 8.5 %copy-start = (f32[64,128]{1,0:T(8,128)S(1)}, f32[64,128]{1,0:T(8,128)}, u32[]{:S(2)}) copy-start(f32[64,128]{1,0:T(8,128)} %param.13) | copy-start | bytes 98308
  47.8 20.2 %copy-start.1 = (s32[64,4]{0,1:T(4,128)S(1)}, s32[64,4]{0,1:T(4,128)}, u32[]{:S(2)}) copy-start(s32[64,4]{0,1:T(4,128)} %param.12) | copy-start | bytes 3076
  48.1 21.7 %collective-permute-start.1 = (f32[256,6,128]{2,0,1:T(8,128)S(1)}, f32[256,6,128]{2,0,1:T(8,128)S(1)}, u32[]{:S(2)}, u32[]{:S(2)}) collective-permute-start(f32[256,6,128]{2,0,1:T(8,128)S(1)} %copy.23), channel_id=1, source_target_pairs={{0,1},{1,0},{2,3},{3,2},{4,5},{5,4},{6,7},{7,6},{8,9},{9,8},{10,11... | collective-permute-start | bytes 2359304 | tf_op jit(solution)/shard_map/ppermute | solution.py:10
  49.9 17.9 %all-to-all-start = ((s32[128,1,2]{2,1,0:T(1,128)}), s32[128,1,2]{2,1,0:T(1,128)S(1)}, u32[]{:S(2)}, u32[]{:S(2)}) async-start(s32[128,1,2]{2,1,0:T(1,128)} %bitcast.1), calls=%async_computation | async-start | bytes 131072 | tf_op jit(solution)/shard_map/all_to_all | solution.py:50
  67.9 1.8 %collective-permute-start = (s32[256]{0:T(256)S(1)}, s32[256]{0:T(256)S(1)}, u32[]{:S(2)}, u32[]{:S(2)}) collective-permute-start(s32[256]{0:T(256)S(1)} %reshape.111), channel_id=1, source_target_pairs={{0,1},{1,0},{2,3},{3,2},{4,5},{5,4},{6,7},{7,6},{8,9},{9,8},{10,11... | collective-permute-start | bytes 3080 | tf_op jit(solution)/shard_map/ppermute | solution.py:10
  85.1 9.8 %collective-permute-start.2 = (bf16[16,6,128]{2,1,0:T(8,128)(2,1)S(1)}, bf16[16,6,128]{2,1,0:T(8,128)(2,1)S(1)}, u32[]{:S(2)}, u32[]{:S(2)}) collective-permute-start(bf16[16,6,128]{2,1,0:T(8,128)(2,1)S(1)} %get-tuple-element.17), channel_id=1, source_target_pairs={{0,1},{1,2},{2,3},{3,4},{4,5},{5,6},{6,7},{7,8},{8,9},{9,10},{10,1... | collective-permute-start | bytes 73736 | tf_op jit(solution)/shard_map/ppermute | solution.py:16
  87.5 9.0 %collective-permute-start.3 = (bf16[16,6,128]{2,1,0:T(8,128)(2,1)S(1)}, bf16[16,6,128]{2,1,0:T(8,128)(2,1)S(1)}, u32[]{:S(2)}, u32[]{:S(2)}) collective-permute-start(bf16[16,6,128]{2,1,0:T(8,128)(2,1)S(1)} %get-tuple-element.18), channel_id=1, source_target_pairs={{1,0},{2,1},{3,2},{4,3},{5,4},{6,5},{7,6},{8,7},{9,8},{10,9},{11,1... | collective-permute-start | bytes 73736 | tf_op jit(solution)/shard_map/ppermute | solution.py:16
where the time goes:
time: 107 us; the launch traced here: 105 us
  blocking collectives  40.7 us (38%)
  local copies, waits for them, and re-layouts  25.5 us (24%)
  starting transfers between devices  16.3 us (15%)
  waiting for transfers between devices  13.1 us (12%)
  matrix products  6.71 us (6%)
  other arithmetic  2.03 us (2%)
    all_to_all x1, blocking collectives, per_device(): lax.all_to_all(outgoing.reshape(n_dom, most, modes, width), 'dom', split_...  40.7 us
    scatter x1, local copies, waits for them, and re-layouts, per_device(): jnp.zeros((rows_dev + 1, modes, width), jnp.float32).at[local]  14.6 us
    all_to_all x1, waiting for transfers between devices, per_device(): lax.all_to_all(send_pos.reshape(n_dom, most), 'dom', split_axis=0, concat...  11.5 us
    ppermute x2, starting transfers between devices, passed_along(): lax.ppermute(value, axis, [(source, source + steps) for source in range(i...  9.78 us
    dot_general x1, matrix products, per_device(): jnp.einsum('tkcj,tkij->tkci', gathered, tiles_a, preferred_element_type=j...  6.71 us
    all_to_all x1, starting transfers between devices, per_device(): lax.all_to_all(send_pos.reshape(n_dom, most), 'dom', split_axis=0, concat...  6.36 us
    scatter x1, local copies, waits for them, and re-layouts, per_device(): jnp.zeros((n_dom * most + 1, modes, width), jnp.float32).at[target]  3.98 us
  transfers between devices with their start and end apart: 5, of which 2 were waited for; matrix products, arithmetic and copies ran while one was open for 3% of the time, Pallas kernels for 0%

commit v1 on v0

v1 whole, which is shorter than its diff:
```python
import jax
import jax.numpy as jnp
from jax import lax
from jax.experimental import pallas as pl
from jax.experimental.pallas import tpu as pltpu
from jax.sharding import PartitionSpec as P

DAMPING = 2.0 / 3.0
BF16 = jnp.bfloat16
F32 = jnp.float32
VMEM = pltpu.VMEM
SMEM = pltpu.SMEM

LANES = 128
MSG_ROWS = 16


def iota(shape, dim):
    return lax.broadcasted_iota(jnp.int32, shape, dim)


def dot(a, b, dims):
    return lax.dot_general(a, b, (dims, ((), ())), preferred_element_type=F32)


def onehot(cond):
    return jnp.where(cond, 1.0, 0.0).astype(BF16)


def pack_kernel(count_ref, agg_ref, pt_ref, out_ref, wide):
    modes, slots, _ = pt_ref.shape
    n_dom = out_ref.shape[0]
    agg = agg_ref[...]
    live = iota((1, slots), 1) < count_ref[0]
    owner = jnp.where(live, agg // LANES, -1)
    position = agg % LANES
    to_dest = owner == iota((n_dom, slots), 0)
    before = onehot(iota((slots, slots), 0) < iota((slots, slots), 1))
    rank = dot(onehot(to_dest), before, ((1,), (0,)))
    first = onehot(to_dest & (rank < 0.5))
    second = onehot(to_dest & (rank > 0.5))
    pick = jnp.concatenate([first, second], axis=0)
    at = onehot(position == iota((LANES, slots), 0))
    where_to = dot(pick, at, ((1,), (1,)))
    blocks = jnp.concatenate([pt_ref[c].astype(BF16) for c in range(modes)], axis=1)
    sent = dot(pick, blocks, ((1,), (0,)))
    for r in range(2):
        rows = slice(r * n_dom, (r + 1) * n_dom)
        for c in range(modes):
            wide[pl.ds(r * modes + c, n_dom, stride=MSG_ROWS), :] = sent[rows, c * LANES : (c + 1) * LANES]
        wide[pl.ds(2 * modes + r, n_dom, stride=MSG_ROWS), :] = where_to[rows]
    for r in range(2 * modes + 2, MSG_ROWS):
        wide[pl.ds(r, n_dom, stride=MSG_ROWS), :] = jnp.zeros((n_dom, LANES), F32)
    out_ref[...] = wide[...].reshape(out_ref.shape).astype(BF16)


def place_kernel(sub_ref, msg_ref, mine_ref, peer_ref, edge_a_ref, edge_b_ref, wide, placed):
    n_dom = msg_ref.shape[0]
    modes = (MSG_ROWS - 2) // 2 - 1
    keep, halo = mine_ref.shape[0], edge_a_ref.shape[0]
    part = LANES
    sub = sub_ref[0]
    wide[...] = msg_ref[...].astype(F32).reshape(wide.shape)

    def column(row):
        return wide[pl.ds(row, n_dom, stride=MSG_ROWS), :].astype(BF16)

    at = jnp.concatenate([column(2 * modes + r) for r in range(2)], axis=0)
    blocks = jnp.concatenate(
        [jnp.concatenate([column(r * modes + c) for c in range(modes)], axis=1) for r in range(2)], axis=0
    )
    placed[...] = dot(at, blocks, ((0,), (0,)))
    low = pl.multiple_of(sub * (part - keep), 16)
    mine_ref[...] = placed[pl.ds(low, keep), :].astype(BF16)
    other = pl.multiple_of((1 - sub) * (part - keep), 16)
    peer_ref[...] = placed[pl.ds(other, keep), :].astype(BF16)
    far = pl.multiple_of((1 - sub) * (part - halo), 16)
    near = pl.multiple_of(sub * (part - halo), 16)
    edge_a_ref[...] = placed[pl.ds(far, halo), :].astype(BF16)
    edge_b_ref[...] = placed[pl.ds(near, halo), :].astype(BF16)


def smooth_kernel(base_ref, cols_ref, mine_ref, peer_ref, edge_a_ref, edge_b_ref, diag_ref, tiles_ref, out_ref, left):
    step = pl.program_id(0)
    n_tile, rows, _ = out_ref.shape
    neigh = tiles_ref.shape[1]
    modes = rows // neigh
    total = cols_ref.shape[1]
    keep, halo = mine_ref.shape[0], edge_a_ref.shape[0]
    n_ext = keep + halo

    @pl.when(step == 0)
    def _():
        ext = jnp.concatenate(
            [mine_ref[...] + peer_ref[...], edge_a_ref[...] + edge_b_ref[...]], axis=0
        )
        local = cols_ref[...] - base_ref[0]
        local = jnp.where(local < 0, local + n_ext, local)
        for k in range(neigh):
            take = onehot(iota((n_ext, total), 0) == local[k : k + 1, :])
            got = dot(take, ext, ((0,), (0,)))
            for c in range(modes):
                left[pl.ds(c * neigh + k, total, stride=rows), :] = got[:, c * LANES : (c + 1) * LANES]

    row_k = iota((rows, LANES), 0) % neigh
    for n in range(n_tile):
        t = step * n_tile + n
        lhs = left[pl.ds(pl.multiple_of(t * rows, 8), rows), :]
        tiles = tiles_ref[n].reshape(neigh * LANES, LANES)
        every = dot(lhs.astype(BF16), tiles, ((1,), (1,)))
        product = every[:, :LANES]
        for k in range(1, neigh):
            product = jnp.where(row_k == k, every[:, k * LANES : (k + 1) * LANES], product)
        scale = -DAMPING * diag_ref[pl.ds(n, 1), :]
        out_ref[n] = scale * product + jnp.where(row_k == 0, lhs, 0.0)


def per_device(pt_old, agg_index, counts, tiles_a, tile_cols, inv_diag):
    n_dom = lax.axis_size("dom")
    n_sub = lax.axis_size("sub")
    slots, modes, width = pt_old.shape
    rows_dev, neigh = tile_cols.shape
    halo = rows_dev // 4
    keep = rows_dev + halo
    sub = lax.axis_index("sub")
    device = lax.axis_index("dom") * n_sub + sub
    vmem = pl.BlockSpec(memory_space=VMEM)
    smem = pl.BlockSpec(memory_space=SMEM)

    messages = pl.pallas_call(
        pack_kernel,
        out_shape=jax.ShapeDtypeStruct((n_dom, MSG_ROWS, width), BF16),
        in_specs=[smem, vmem, vmem],
        out_specs=vmem,
        scratch_shapes=[VMEM((n_dom * MSG_ROWS, width), F32)],
        name="pack",
    )(counts, agg_index.reshape(1, slots), jnp.transpose(pt_old, (1, 0, 2)))

    arrived = lax.all_to_all(messages, "dom", split_axis=0, concat_axis=0, tiled=True)

    flat = modes * width
    mine, for_peer, edge_a, edge_b = pl.pallas_call(
        place_kernel,
        out_shape=[jax.ShapeDtypeStruct((n, flat), BF16) for n in (keep, keep, halo, halo)],
        in_specs=[smem, vmem],
        out_specs=[vmem] * 4,
        scratch_shapes=[VMEM((n_dom * MSG_ROWS, width), F32), VMEM((LANES, flat), F32)],
        name="place",
    )(sub.reshape(1), arrived)

    n_dev = n_dom * n_sub
    both = ("dom", "sub")
    peer = lax.ppermute(for_peer, both, [(i, i ^ 1) for i in range(n_dev)])
    same, cross = [], []
    for p in range(n_dom):
        if p + 1 < n_dom:
            same.append((2 * p, 2 * p + 2))
            cross.append((2 * p + 1, 2 * p + 2))
        if p > 0:
            same.append((2 * p + 1, 2 * p - 1))
            cross.append((2 * p, 2 * p - 1))
    edge_a = lax.ppermute(edge_a, both, same)
    edge_b = lax.ppermute(edge_b, both, cross)

    base = device * rows_dev - sub * halo
    per_step = 8
    whole = lambda shape: pl.BlockSpec(shape, lambda i: (0,) * len(shape))
    out = pl.pallas_call(
        smooth_kernel,
        out_shape=jax.ShapeDtypeStruct((rows_dev, modes * neigh, width), F32),
        grid=(rows_dev // per_step,),
        in_specs=[
            smem,
            whole((neigh, rows_dev)),
            whole((keep, flat)),
            whole((keep, flat)),
            whole((halo, flat)),
            whole((halo, flat)),
            pl.BlockSpec((per_step, width), lambda i: (i, 0)),
            pl.BlockSpec((per_step, neigh, width, width), lambda i: (i, 0, 0, 0)),
        ],
        out_specs=pl.BlockSpec((per_step, modes * neigh, width), lambda i: (i, 0, 0)),
        scratch_shapes=[VMEM((rows_dev * modes * neigh, width), F32)],
        name="smooth",
    )(base.reshape(1), tile_cols.T, mine, peer, edge_a, edge_b, inv_diag, tiles_a)
    return jnp.transpose(out.reshape(rows_dev, modes, neigh, width), (0, 2, 1, 3))


def solution(mesh):
    in_specs = (
        P(("dom", "sub"), None, None),
        P(("dom", "sub")),
        P(("dom", "sub")),
        P(("dom", "sub"), None, None, None),
        P(("dom", "sub"), None),
        P(("dom", "sub"), None),
    )
    out_specs = P(("dom", "sub"), None, None, None)
    return jax.shard_map(
        per_device, mesh=mesh, in_specs=in_specs, out_specs=out_specs, check_vma=False
    )
```

time: 107 us -> 63.4 us (0.59); the launches traced: 105 us -> 63 us
  blocking collectives: 40.7 us -> 0 us
  local copies, waits for them, and re-layouts: 25.5 us -> 1.44 us
  Pallas kernels: 0 us -> 13.5 us
  waiting for transfers between devices: 13.1 us -> 26.2 us
  matrix products: 6.71 us -> 0 us
  starting transfers between devices: 16.3 us -> 21.1 us
  other arithmetic: 2.03 us -> 0 us
    all_to_all x1 -> x0, blocking collectives: 40.7 us -> none  [per_device(): lax.all_to_all(outgoing.reshape(n_dom, most, modes, width), 'dom', split_...]
    scatter x3 -> x0, local copies, waits for them, and re-layouts: 19.5 us -> none  [the longest x1 14.6 us: per_device(): jnp.zeros((rows_dev + 1, modes, width), jnp.float32).at[local]]
    pallas_call x0 -> x3, Pallas kernels: none -> 13.5 us  [the longest x1 8.82 us: per_device(): pl.pallas_call(smooth_kernel, out_shape=jax.ShapeDtypeStruct((rows_dev, m...]
    all_to_all x1, waiting for transfers between devices: 11.5 us -> 20.3 us  [per_device(): lax.all_to_all(messages, 'dom', split_axis=0, concat_axis=0, tiled=True)]
    all_to_all x1, starting transfers between devices: 6.36 us -> 15 us  [per_device(): lax.all_to_all(messages, 'dom', split_axis=0, concat_axis=0, tiled=True)]
    dot_general x1 -> x0, matrix products: 6.71 us -> none  [per_device(): jnp.einsum('tkcj,tkij->tkci', gathered, tiles_a, preferred_element_type=j...]
    ppermute x4 -> x3, waiting for transfers between devices: 1.56 us -> 5.9 us  [the longest x1 3.99 us: per_device(): edge_a = lax.ppermute(edge_a, both, same)]
    ppermute x4 -> x3, starting transfers between devices: 9.97 us -> 6.12 us  [the longest x1 3.65 us: per_device(): edge_b = lax.ppermute(edge_b, both, cross)]
  transfers between devices with their start and end apart: 5 -> 4, of which waited for: 2 -> 3; matrix products, arithmetic and copies ran while one was open for 3% -> 0% of each run, Pallas kernels for 0% -> 0%
where the time goes in v1:
time: 63.4 us; the launch traced here: 63 us
  waiting for transfers between devices  26.2 us (41%)
  starting transfers between devices  21.1 us (33%)
  Pallas kernels  13.5 us (21%)
  local copies, waits for them, and re-layouts  1.44 us (2%)
  between operations  0.7 us (1%)
    all_to_all x1, waiting for transfers between devices, per_device(): lax.all_to_all(messages, 'dom', split_axis=0, concat_axis=0, tiled=True)  20.3 us
    all_to_all x1, starting transfers between devices, per_device(): lax.all_to_all(messages, 'dom', split_axis=0, concat_axis=0, tiled=True)  15 us
    pallas_call x1, Pallas kernels, per_device(): pl.pallas_call(smooth_kernel, out_shape=jax.ShapeDtypeStruct((rows_dev, m...  8.82 us
    ppermute x1, waiting for transfers between devices, per_device(): edge_a = lax.ppermute(edge_a, both, same)  3.99 us
    ppermute x1, starting transfers between devices, per_device(): edge_b = lax.ppermute(edge_b, both, cross)  3.65 us
    ppermute x1, starting transfers between devices, per_device(): edge_a = lax.ppermute(edge_a, both, same)  2.47 us
    pallas_call x1, Pallas kernels, per_device(): pl.pallas_call(pack_kernel, out_shape=jax.ShapeDtypeStruct((n_dom, MSG_RO...  2.45 us
    pallas_call x1, Pallas kernels, per_device(): pl.pallas_call(place_kernel, out_shape=[jax.ShapeDtypeStruct((n, flat), B...  2.21 us
  transfers between devices with their start and end apart: 4, of which 3 were waited for; matrix products, arithmetic and copies ran while one was open for 0% of the time, Pallas kernels for 0%

profile of v1, /device:TPU:32, one launch (start us, length us, event | category | flops | bytes accessed | tf_op | source)
XLA Modules:
  0.0 63.0 jit_solution(5644937788618657261)
XLA Ops:
  0.7 2.4 %pack.1 = bf16[128,16,128]{2,1,0:T(8,128)(2,1)} custom-call(s32[1]{0:T(128)S(6)} %copy.7.count_ref, s32[1,104]{1,0:T(1,128)} %bitcast.10, f32[6,104,128]{2,1,0:T(8,128)} %bitcast.8), custom_call_target="tpu_custom_call" | custom-call | tf_op jit(solution)/shard_map/pack/pallas_call | solution.py:130
  3.1 15.0 %all-to-all-start = ((bf16[128,16,128]{2,1,0:T(8,128)(2,1)}), bf16[128,16,128]{2,1,0:T(8,128)(2,1)S(1)}, u32[]{:S(2)}, u32[]{:S(2)}) async-start(bf16[128,16,128]{2,1,0:T(8,128)(2,1)} %pack.1), calls=%async_computation | async-start | bytes 1048576 | tf_op jit(solution)/shard_map/all_to_all | solution.py:139
  18.1 20.3 %all-to-all-done.msg_ref = bf16[128,16,128]{2,1,0:T(8,128)(2,1)S(1)} async-done(((bf16[128,16,128]{2,1,0:T(8,128)(2,1)}), bf16[128,16,128]{2,1,0:T(8,128)(2,1)S(1)}, u32[]{:S(2)}, u32[]{:S(2)}) %all-to-all-start) | async-done | bytes 524320 | tf_op jit(solution)/shard_map/all_to_all | solution.py:139
  38.4 0.0 copy-start
  38.4 0.8 %copy-done = bf16[128,16,128]{2,1,0:T(8,128)(2,1)} copy-done((bf16[128,16,128]{2,1,0:T(8,128)(2,1)}, bf16[128,16,128]{2,1,0:T(8,128)(2,1)S(1)}, u32[]{:S(2)}) %copy-start) | copy-done | bytes 524312
  39.2 2.2 %place.1 = (bf16[80,768]{1,0:T(8,128)(2,1)}, bf16[80,768]{1,0:T(8,128)(2,1)}, bf16[16,768]{1,0:T(8,128)(2,1)}, bf16[16,768]{1,0:T(8,128)(2,1)}) custom-call(s32[1]{0:T(128)} %bitcast.2.sub_ref, bf16[128,16,128]{2,1,0:T(8,128)(2,1)} %copy-done), custom_call_target="tpu_custom_call" | custom-call | tf_op jit(solution)/shard_map/place/pallas_call | solution.py:142
  41.4 0.0 collective-permute-start
  41.5 2.5 %collective-permute-start.1 = (bf16[16,768]{1,0:T(8,128)(2,1)}, bf16[16,768]{1,0:T(8,128)(2,1)S(1)}, u32[]{:S(2)}, u32[]{:S(2)}) collective-permute-start(bf16[16,768]{1,0:T(8,128)(2,1)} %get-tuple-element.11), channel_id=1, source_target_pairs={{0,2},{2,4},{3,1},{4,6},{5,3},{6,8},{7,5},{8,10},{9,7},{10,12},{11... | collective-permute-start | bytes 73736 | tf_op jit(solution)/shard_map/ppermute | solution.py:162
  43.9 3.7 %collective-permute-start.2 = (bf16[16,768]{1,0:T(8,128)(2,1)}, bf16[16,768]{1,0:T(8,128)(2,1)S(1)}, u32[]{:S(2)}, u32[]{:S(2)}) collective-permute-start(bf16[16,768]{1,0:T(8,128)(2,1)} %get-tuple-element.12), channel_id=1, source_target_pairs={{1,2},{3,4},{2,1},{5,6},{4,3},{7,8},{6,5},{9,10},{8,7},{11,12},{10... | collective-permute-start | bytes 73736 | tf_op jit(solution)/shard_map/ppermute | solution.py:163
  47.6 4.0 %collective-permute-done.1.edge_a_ref = bf16[16,768]{1,0:T(8,128)(2,1)S(1)} collective-permute-done((bf16[16,768]{1,0:T(8,128)(2,1)}, bf16[16,768]{1,0:T(8,128)(2,1)S(1)}, u32[]{:S(2)}, u32[]{:S(2)}) %collective-permute-start.1) | collective-permute-done | bytes 24608 | tf_op jit(solution)/shard_map/ppermute | solution.py:162
  51.6 0.0 copy-start.2
  51.6 1.9 %collective-permute-done.2.edge_b_ref = bf16[16,768]{1,0:T(8,128)(2,1)S(1)} collective-permute-done((bf16[16,768]{1,0:T(8,128)(2,1)}, bf16[16,768]{1,0:T(8,128)(2,1)S(1)}, u32[]{:S(2)}, u32[]{:S(2)}) %collective-permute-start.2) | collective-permute-done | bytes 24608 | tf_op jit(solution)/shard_map/ppermute | solution.py:163
  53.5 0.0 copy-start.3
  53.5 0.0 collective-permute-done.peer_ref
  53.5 0.0 copy-start.1
  53.5 0.0 copy-done.2
  53.5 0.6 copy-done.3
  54.1 0.1 copy-done.1
  54.2 8.8 %smooth.1 = f32[64,24,128]{2,1,0:T(8,128)} custom-call(s32[1]{0:T(128)} %bitcast.base_ref, s32[4,64]{1,0:T(4,128)} %bitcast.9, bf16[80,768]{1,0:T(8,128)(2,1)} %get-tuple-element.9.mine_ref, bf16[80,768]{1,0:T(8,128)(2,1)} %copy-done.1, bf16[16,768]{1,0:T(8,128)(2,1)} %copy-done.2, bf16[16,768]{1,0:T(8,128)(2,1)} %copy-done.3, f32[64,128]{1,0:T(8,128)} %diag_ref.1, ...), custom_call_target="tpu_custom_call" | custom-call | tf_op jit(solution)/shard_map/smooth/pallas_call | solution.py:168
Async XLA Ops:
  3.1 35.3 %all-to-all-start = ((bf16[128,16,128]{2,1,0:T(8,128)(2,1)}), bf16[128,16,128]{2,1,0:T(8,128)(2,1)S(1)}, u32[]{:S(2)}, u32[]{:S(2)}) async-start(bf16[128,16,128]{2,1,0:T(8,128)(2,1)} %pack.1), calls=%async_computation | async-start | bytes 1048576 | tf_op jit(solution)/shard_map/all_to_all | solution.py:139
  38.4 0.8 %copy-start = (bf16[128,16,128]{2,1,0:T(8,128)(2,1)}, bf16[128,16,128]{2,1,0:T(8,128)(2,1)S(1)}, u32[]{:S(2)}) copy-start(bf16[128,16,128]{2,1,0:T(8,128)(2,1)S(1)} %all-to-all-done.msg_ref) | copy-start | bytes 1572868
  41.4 12.1 %collective-permute-start = (bf16[80,768]{1,0:T(8,128)(2,1)}, bf16[80,768]{1,0:T(8,128)(2,1)S(1)}, u32[]{:S(2)}, u32[]{:S(2)}) collective-permute-start(bf16[80,768]{1,0:T(8,128)(2,1)} %get-tuple-element.10), channel_id=1, source_target_pairs={{0,1},{1,0},{2,3},{3,2},{4,5},{5,4},{6,7},{7,6},{8,9},{9,8},{10,11... | collective-permute-start | bytes 368648 | tf_op jit(solution)/shard_map/ppermute | solution.py:153
  41.5 10.1 %collective-permute-start.1 = (bf16[16,768]{1,0:T(8,128)(2,1)}, bf16[16,768]{1,0:T(8,128)(2,1)S(1)}, u32[]{:S(2)}, u32[]{:S(2)}) collective-permute-start(bf16[16,768]{1,0:T(8,128)(2,1)} %get-tuple-element.11), channel_id=1, source_target_pairs={{0,2},{2,4},{3,1},{4,6},{5,3},{6,8},{7,5},{8,10},{9,7},{10,12},{11... | collective-permute-start | bytes 73736 | tf_op jit(solution)/shard_map/ppermute | solution.py:162
  43.9 9.6 %collective-permute-start.2 = (bf16[16,768]{1,0:T(8,128)(2,1)}, bf16[16,768]{1,0:T(8,128)(2,1)S(1)}, u32[]{:S(2)}, u32[]{:S(2)}) collective-permute-start(bf16[16,768]{1,0:T(8,128)(2,1)} %get-tuple-element.12), channel_id=1, source_target_pairs={{1,2},{3,4},{2,1},{5,6},{4,3},{7,8},{6,5},{9,10},{8,7},{11,12},{10... | collective-permute-start | bytes 73736 | tf_op jit(solution)/shard_map/ppermute | solution.py:163
  51.6 1.9 %copy-start.2 = (bf16[16,768]{1,0:T(8,128)(2,1)}, bf16[16,768]{1,0:T(8,128)(2,1)S(1)}, u32[]{:S(2)}) copy-start(bf16[16,768]{1,0:T(8,128)(2,1)S(1)} %collective-permute-done.1.edge_a_ref) | copy-start | bytes 73732
  53.5 0.6 copy-start.3
  53.5 0.7 %copy-start.1 = (bf16[80,768]{1,0:T(8,128)(2,1)}, bf16[80,768]{1,0:T(8,128)(2,1)S(1)}, u32[]{:S(2)}) copy-start(bf16[80,768]{1,0:T(8,128)(2,1)S(1)} %collective-permute-done.peer_ref) | copy-start | bytes 368644

commit v2 on v1

v2 whole, which is shorter than its diff:
```python
import jax
import jax.numpy as jnp
from jax import lax
from jax.experimental import pallas as pl
from jax.experimental.pallas import tpu as pltpu
from jax.sharding import PartitionSpec as P

DAMPING = 2.0 / 3.0
BF16 = jnp.bfloat16
F32 = jnp.float32
VMEM = pltpu.VMEM
SMEM = pltpu.SMEM

LANES = 128
MIB = 2**20
PARAMS = pltpu.CompilerParams(vmem_limit_bytes=20 * MIB)
WIDE = pltpu.CompilerParams(vmem_limit_bytes=60 * MIB)
MSG_ROWS = 14


def iota(shape, dim):
    return lax.broadcasted_iota(jnp.int32, shape, dim)


def dot(a, b, dims):
    return lax.dot_general(a, b, (dims, ((), ())), preferred_element_type=F32)


def onehot(cond):
    return jnp.where(cond, 1.0, 0.0).astype(BF16)


def pack_kernel(count_hbm, agg_hbm, pt_hbm, out_ref, wide, count_ref, agg_ref, pt_ref, sems):
    modes, slots, _ = pt_ref.shape
    n_dom = out_ref.shape[0] // MSG_ROWS
    copies = [
        pltpu.make_async_copy(count_hbm, count_ref, sems.at[0]),
        pltpu.make_async_copy(agg_hbm, agg_ref, sems.at[1]),
        pltpu.make_async_copy(pt_hbm, pt_ref, sems.at[2]),
    ]
    for copy in copies:
        copy.start()
    copies[0].wait()
    copies[1].wait()
    agg = agg_ref[...]
    live = iota((1, slots), 1) < count_ref[0]
    owner = jnp.where(live, agg // LANES, -1)
    position = agg % LANES
    to_dest = owner == iota((n_dom, slots), 0)
    before = onehot(iota((slots, slots), 0) < iota((slots, slots), 1))
    rank = dot(onehot(to_dest), before, ((1,), (0,)))
    first = onehot(to_dest & (rank < 0.5))
    second = onehot(to_dest & (rank > 0.5))
    pick = jnp.concatenate([first, second], axis=0)
    at = onehot(position == iota((LANES, slots), 0))
    where_to = dot(pick, at, ((1,), (1,)))
    copies[2].wait()
    blocks = jnp.concatenate([pt_ref[c].astype(BF16) for c in range(modes)], axis=1)
    sent = dot(pick, blocks, ((1,), (0,)))
    for r in range(2):
        rows = slice(r * n_dom, (r + 1) * n_dom)
        for c in range(modes):
            wide[pl.ds(r * modes + c, n_dom, stride=MSG_ROWS), :] = sent[rows, c * LANES : (c + 1) * LANES]
        wide[pl.ds(2 * modes + r, n_dom, stride=MSG_ROWS), :] = where_to[rows]
    out_ref[...] = wide[...].astype(BF16)


def place_kernel(sub_ref, msg_ref, mine_ref, peer_ref, wide, placed):
    n_dom = msg_ref.shape[0] // MSG_ROWS
    modes = MSG_ROWS // 2 - 1
    keep = mine_ref.shape[0]
    sub = sub_ref[0]
    wide[...] = msg_ref[...].astype(F32)

    def column(row):
        return wide[pl.ds(row, n_dom, stride=MSG_ROWS), :].astype(BF16)

    at = jnp.concatenate([column(2 * modes + r) for r in range(2)], axis=0)
    blocks = jnp.concatenate(
        [jnp.concatenate([column(r * modes + c) for c in range(modes)], axis=1) for r in range(2)], axis=0
    )
    placed[...] = dot(at, blocks, ((0,), (0,)))
    low = pl.multiple_of(sub * (LANES - keep), 16)
    mine_ref[...] = placed[pl.ds(low, keep), :].astype(BF16)
    other = pl.multiple_of((1 - sub) * (LANES - keep), 16)
    peer_ref[...] = placed[pl.ds(other, keep), :].astype(BF16)


def edge_kernel(sub_ref, mine_ref, peer_ref, edge_ref):
    keep, halo = mine_ref.shape[0], edge_ref.shape[0]
    low = pl.multiple_of(sub_ref[0] * (keep - halo), 16)
    edge_ref[...] = mine_ref[pl.ds(low, halo), :] + peer_ref[pl.ds(low, halo), :]


def turn_kernel(tiles_ref, out_ref):
    n_tile, neigh, width, _ = tiles_ref.shape
    for n in range(n_tile):
        for k in range(neigh):
            out_ref[n, k * width : (k + 1) * width, :] = tiles_ref[n, k].T


def gather(ext, local, left, neigh, modes):
    total = local.shape[1]
    for k in range(neigh):
        take = onehot(iota((ext.shape[0], total), 0) == local[k : k + 1, :])
        got = dot(take, ext, ((0,), (0,)))
        for c in range(modes):
            left[pl.ds(c * neigh + k, total, stride=modes * neigh), :] = got[:, c * LANES : (c + 1) * LANES]


def smooth_row(t, left, tiles, diag_ref, neigh, rows):
    lhs = left[pl.ds(pl.multiple_of(t * rows, 8), rows), :]
    row_k = iota((rows, LANES), 0) % neigh
    spread = jnp.concatenate([jnp.where(row_k == k, lhs, 0.0).astype(BF16) for k in range(neigh)], axis=1)
    product = dot(spread, tiles, ((1,), (0,)))
    scale = -DAMPING * diag_ref[pl.ds(t, 1), :]
    return scale * product + jnp.where(row_k == 0, lhs, 0.0)


def inner_kernel(
    sub_ref, base_ref, cols_ref, mine_ref, peer_ref, diag_ref, tiles_hbm, out_hbm, rest_ref, left, tiles, done, in_sems, out_sems
):
    count, rows, _ = done.shape
    neigh, total = cols_ref.shape
    rest = total - count
    modes = rows // neigh
    chunk = count // (in_sems.shape[0] - 1)
    sub = sub_ref[0]
    start = (1 - sub) * rest

    fetches = []
    for i in range(count // chunk):
        place = pl.ds(i * chunk, chunk)
        fetches.append(pltpu.make_async_copy(tiles_hbm.at[pl.ds(start + i * chunk, chunk)], tiles.at[place], in_sems.at[i]))
    fetches.append(pltpu.make_async_copy(tiles_hbm.at[pl.ds(sub * count, rest)], rest_ref, in_sems.at[count // chunk]))
    for fetch in fetches:
        fetch.start()

    gather(mine_ref[...] + peer_ref[...], cols_ref[...] - base_ref[0], left, neigh, modes)

    writes = []
    for i in range(count // chunk):
        fetches[i].wait()
        for n in range(i * chunk, (i + 1) * chunk):
            done[n] = smooth_row(start + n, left, tiles[n], diag_ref, neigh, rows)
        place = pl.ds(i * chunk, chunk)
        writes.append(pltpu.make_async_copy(done.at[place], out_hbm.at[pl.ds(start + i * chunk, chunk)], out_sems.at[i]))
        writes[-1].start()
    fetches[-1].wait()
    for write in writes:
        write.wait()


def outer_kernel(
    sub_ref, base_ref, cols_ref, mine_ref, peer_ref, edge_ref, diag_ref, rest_ref, begun_hbm, out_hbm, left, done, sem
):
    del begun_hbm
    rest, rows, _ = done.shape
    neigh, total = cols_ref.shape
    modes = rows // neigh
    start = sub_ref[0] * (total - rest)
    ext = jnp.concatenate([mine_ref[...] + peer_ref[...], edge_ref[...]], axis=0)
    local = cols_ref[...] - base_ref[0]
    gather(ext, jnp.where(local < 0, local + ext.shape[0], local), left, neigh, modes)
    for n in range(rest):
        done[n] = smooth_row(start + n, left, rest_ref[n], diag_ref, neigh, rows)
    write = pltpu.make_async_copy(done, out_hbm.at[pl.ds(start, rest)], sem)
    write.start()
    write.wait()


def per_device(pt_old, agg_index, counts, tiles_a, tile_cols, inv_diag):
    n_dom = lax.axis_size("dom")
    n_sub = lax.axis_size("sub")
    slots, modes, width = pt_old.shape
    rows_dev, neigh = tile_cols.shape
    halo = rows_dev // 4
    keep = rows_dev + halo
    sub = lax.axis_index("sub")
    device = lax.axis_index("dom") * n_sub + sub
    vmem = pl.BlockSpec(memory_space=VMEM)
    smem = pl.BlockSpec(memory_space=SMEM)

    hbm = pl.BlockSpec(memory_space=pl.ANY)
    flat = modes * width
    msg_shape = (n_dom * MSG_ROWS, width)
    messages = pl.pallas_call(
        pack_kernel,
        out_shape=jax.ShapeDtypeStruct(msg_shape, BF16),
        in_specs=[hbm, hbm, hbm],
        out_specs=vmem,
        scratch_shapes=[
            VMEM(msg_shape, F32),
            SMEM((1,), jnp.int32),
            VMEM((1, slots), jnp.int32),
            VMEM((modes, slots, width), F32),
            pltpu.SemaphoreType.DMA((3,)),
        ],
        compiler_params=WIDE,
        name="pack",
    )(counts, agg_index.reshape(1, slots), jnp.transpose(pt_old, (1, 0, 2)))

    messages, tiles_a = lax.optimization_barrier((messages, tiles_a))
    arrived = lax.all_to_all(
        messages.reshape(n_dom, MSG_ROWS // 2, 2, width), "dom", split_axis=0, concat_axis=0, tiled=True
    ).reshape(msg_shape)

    per_step = 16
    turned = pl.pallas_call(
        turn_kernel,
        out_shape=jax.ShapeDtypeStruct((rows_dev, neigh * width, width), BF16),
        grid=(rows_dev // per_step,),
        in_specs=[pl.BlockSpec((per_step, neigh, width, width), lambda i: (i, 0, 0, 0))],
        out_specs=pl.BlockSpec((per_step, neigh * width, width), lambda i: (i, 0, 0)),
        compiler_params=WIDE,
        cost_estimate=pl.CostEstimate(flops=0, bytes_accessed=2 * tiles_a.size * 2, transcendentals=0),
        name="turn",
    )(tiles_a)
    arrived, turned = lax.optimization_barrier((arrived, turned))

    mine, for_peer = pl.pallas_call(
        place_kernel,
        out_shape=[jax.ShapeDtypeStruct((keep, flat), BF16)] * 2,
        in_specs=[smem, vmem],
        out_specs=[vmem] * 2,
        scratch_shapes=[VMEM(msg_shape, F32), VMEM((LANES, flat), F32)],
        compiler_params=PARAMS,
        name="place",
    )(sub.reshape(1), arrived)

    n_dev = n_dom * n_sub
    both = ("dom", "sub")
    peer = lax.ppermute(for_peer, both, [(i, i ^ 1) for i in range(n_dev)])
    edge = pl.pallas_call(
        edge_kernel,
        out_shape=jax.ShapeDtypeStruct((halo, flat), BF16),
        in_specs=[smem, vmem, vmem],
        out_specs=vmem,
        compiler_params=PARAMS,
        name="edge",
    )(sub.reshape(1), mine, peer)
    across = [pair for i in range(1, n_dev - 1, 2) for pair in ((i, i + 1), (i + 1, i))]
    edge = lax.ppermute(edge, both, across)

    base = device * rows_dev - sub * halo
    rows = modes * neigh
    inner = rows_dev - halo
    chunk = 8
    out_shape = jax.ShapeDtypeStruct((rows_dev, rows, width), F32)
    left_shape = VMEM((rows_dev * rows, width), F32)
    begun, rest = pl.pallas_call(
        inner_kernel,
        out_shape=[out_shape, jax.ShapeDtypeStruct((halo, neigh * width, width), BF16)],
        in_specs=[smem, smem] + [vmem] * 4 + [hbm],
        out_specs=[hbm, vmem],
        scratch_shapes=[
            left_shape,
            VMEM((inner, neigh * width, width), BF16),
            VMEM((inner, rows, width), F32),
            pltpu.SemaphoreType.DMA((inner // chunk + 1,)),
            pltpu.SemaphoreType.DMA((inner // chunk,)),
        ],
        compiler_params=pltpu.CompilerParams(vmem_limit_bytes=48 * MIB),
        cost_estimate=pl.CostEstimate(
            flops=2 * inner * rows * neigh * width * width, bytes_accessed=tiles_a.size * 2, transcendentals=0
        ),
        name="inner",
    )(sub.reshape(1), base.reshape(1), tile_cols.T, mine, peer, inv_diag, turned)
    out = pl.pallas_call(
        outer_kernel,
        out_shape=out_shape,
        in_specs=[smem, smem] + [vmem] * 6 + [hbm],
        out_specs=hbm,
        scratch_shapes=[left_shape, VMEM((halo, rows, width), F32), pltpu.SemaphoreType.DMA],
        input_output_aliases={8: 0},
        compiler_params=PARAMS,
        name="outer",
    )(sub.reshape(1), base.reshape(1), tile_cols.T, mine, peer, edge, inv_diag, rest, begun)
    return jnp.transpose(out.reshape(rows_dev, modes, neigh, width), (0, 2, 1, 3))


def solution(mesh):
    in_specs = (
        P(("dom", "sub"), None, None),
        P(("dom", "sub")),
        P(("dom", "sub")),
        P(("dom", "sub"), None, None, None),
        P(("dom", "sub"), None),
        P(("dom", "sub"), None),
    )
    out_specs = P(("dom", "sub"), None, None, None)
    return jax.shard_map(
        per_device, mesh=mesh, in_specs=in_specs, out_specs=out_specs, check_vma=False
    )
```

time: 63.4 us -> 49.5 us (0.78)
  waiting for transfers between devices: 26.2 us -> 14.8 us
  starting transfers between devices: 21.1 us -> 18.1 us
  Pallas kernels: 13.5 us -> 15.7 us
  local copies, waits for them, and re-layouts: 1.44 us -> 0.01 us
    all_to_all x1, waiting for transfers between devices: 20.3 us -> 11 us  [per_device(): lax.all_to_all(messages.reshape(n_dom, MSG_ROWS // 2, 2, width), 'dom', s...]
    ppermute x2 -> x1, waiting for transfers between devices: 5.9 us -> 2.45 us  [per_device(): edge = lax.ppermute(edge, both, across)]
    ppermute x2 -> x1, starting transfers between devices: 6.12 us -> 2.94 us  [per_device(): edge = lax.ppermute(edge, both, across)]
    pallas_call x3 -> x6, Pallas kernels: 13.5 us -> 15.7 us  [the longest x1 7.9 us: per_device(): pl.pallas_call(turn_kernel, out_shape=jax.ShapeDtypeStruct((rows_dev, nei...]
    unnamed x8 -> x4, local copies, waits for them, and re-layouts: 1.44 us -> 0.01 us
    ppermute x1, waiting for transfers between devices: 0.01 us -> 1.32 us  [per_device(): peer = lax.ppermute(for_peer, both, [(i, i ^ 1) for i in range(n_dev)])]
  transfers between devices with their start and end apart: 4 -> 3, of which waited for: 3 -> 3; matrix products, arithmetic and copies ran while one was open for 0% -> 0% of each run, Pallas kernels for 0% -> 24%
where the time goes in v2:
time: 49.5 us; the launch traced here: 49.3 us
  starting transfers between devices  18.1 us (37%)
  Pallas kernels  15.7 us (32%)
  waiting for transfers between devices  14.8 us (30%)
  between operations  0.75 us (2%)
    all_to_all x1, starting transfers between devices, per_device(): lax.all_to_all(messages.reshape(n_dom, MSG_ROWS // 2, 2, width), 'dom', s...  15 us
    all_to_all x1, waiting for transfers between devices, per_device(): lax.all_to_all(messages.reshape(n_dom, MSG_ROWS // 2, 2, width), 'dom', s...  11 us
    pallas_call x1, Pallas kernels, per_device(): pl.pallas_call(turn_kernel, out_shape=jax.ShapeDtypeStruct((rows_dev, nei...  7.9 us
    pallas_call x1, Pallas kernels, per_device(): pl.pallas_call(inner_kernel, out_shape=[out_shape, jax.ShapeDtypeStruct((...  3.92 us
    ppermute x1, starting transfers between devices, per_device(): edge = lax.ppermute(edge, both, across)  2.94 us
    ppermute x1, waiting for transfers between devices, per_device(): edge = lax.ppermute(edge, both, across)  2.45 us
    pallas_call x1, Pallas kernels, per_device(): pl.pallas_call(pack_kernel, out_shape=jax.ShapeDtypeStruct(msg_shape, BF1...  2.08 us
    pallas_call x1, Pallas kernels, per_device(): pl.pallas_call(outer_kernel, out_shape=out_shape, in_specs=[smem, smem] +...  1.43 us
  transfers between devices with their start and end apart: 3, of which 3 were waited for; matrix products, arithmetic and copies ran while one was open for 0% of the time, Pallas kernels for 24%

profile of v2, /device:TPU:32, one launch (start us, length us, event | category | flops | bytes accessed | tf_op | source)
XLA Modules:
  0.0 49.3 jit_solution(1384759404862814499)
XLA Ops:
  0.7 2.1 %pack.1 = bf16[1792,128]{1,0:T(8,128)(2,1)} custom-call(s32[1]{0:T(128)S(6)} %copy.9.count_hbm, s32[1,104]{1,0:T(1,128)} %bitcast.15, f32[6,104,128]{2,1,0:T(8,128)} %bitcast.14), custom_call_target="tpu_custom_call" | custom-call | tf_op jit(solution)/shard_map/pack/pallas_call | solution.py:187
  2.7 15.0 %all-to-all-start = ((bf16[128,7,2,128]{3,2,1,0:T(2,128)(2,1)}), bf16[128,7,2,128]{3,2,1,0:T(2,128)(2,1)S(1)}, u32[]{:S(2)}, u32[]{:S(2)}) async-start(bf16[128,7,2,128]{3,2,1,0:T(2,128)(2,1)} %bitcast.13), calls=%async_computation | async-start | bytes 917504 | tf_op jit(solution)/shard_map/all_to_all | solution.py:204
  17.8 0.0 copy-start
  17.8 0.0 copy-start.1
  17.8 7.9 %turn.1.tiles_hbm = bf16[64,512,128]{2,1,0:T(8,128)(2,1)} custom-call(bf16[64,4,128,128]{3,2,1,0:T(8,128)(2,1)} %tiles_ref), custom_call_target="tpu_custom_call" | custom-call | bytes 16777216 | tf_op jit(solution)/shard_map/turn/pallas_call | solution.py:209
  25.7 11.0 %all-to-all-done = bf16[128,7,2,128]{3,2,1,0:T(2,128)(2,1)S(1)} async-done(((bf16[128,7,2,128]{3,2,1,0:T(2,128)(2,1)}), bf16[128,7,2,128]{3,2,1,0:T(2,128)(2,1)S(1)}, u32[]{:S(2)}, u32[]{:S(2)}) %all-to-all-start) | async-done | bytes 458784 | tf_op jit(solution)/shard_map/all_to_all | solution.py:204
  36.7 0.3 place.1
  37.0 0.1 collective-permute-start
  37.1 1.3 %collective-permute-done.peer_ref = bf16[80,768]{1,0:T(8,128)(2,1)S(1)} collective-permute-done((bf16[80,768]{1,0:T(8,128)(2,1)S(1)}, bf16[80,768]{1,0:T(8,128)(2,1)S(1)}, u32[]{:S(2)}, u32[]{:S(2)}) %collective-permute-start) | collective-permute-done | bytes 122912 | tf_op jit(solution)/shard_map/ppermute | solution.py:233
  38.5 2.9 %collective-permute-start.1 = (bf16[16,768]{1,0:T(8,128)(2,1)S(1)}, bf16[16,768]{1,0:T(8,128)(2,1)S(1)}, u32[]{:S(2)}, u32[]{:S(2)}) collective-permute-start(bf16[16,768]{1,0:T(8,128)(2,1)S(1)} %edge.1), channel_id=1, source_target_pairs={{1,2},{2,1},{3,4},{4,3},{5,6},{6,5},{7,8},{8,7},{9,10},{10,9},{11,... | collective-permute-start | bytes 73736 | tf_op jit(solution)/shard_map/ppermute | solution.py:243
  41.4 0.0 copy-done
  41.4 0.0 copy-done.1
  41.5 3.9 %inner.1 = (f32[64,24,128]{2,1,0:T(8,128)}, bf16[16,512,128]{2,1,0:T(8,128)(2,1)S(1)}) custom-call(s32[1]{0:T(128)} %bitcast.sub_ref, s32[1]{0:T(128)} %bitcast.1.base_ref, s32[4,64]{1,0:T(4,128)S(1)} %bitcast.11, bf16[80,768]{1,0:T(8,128)(2,1)S(1)} %get-tuple-element.16.mine_ref, bf16[80,768]{1,0:T(8,128)(2,1)S(1)} %collective-permute-done.peer_ref, ...), custom_call_target="tpu_custom_call" | custom-call | flops 150994944 | bytes 8388608 | tf_op jit(solution)/shard_map/inner/pallas_call | solution.py:251
  45.4 2.4 %collective-permute-done.1.edge_ref = bf16[16,768]{1,0:T(8,128)(2,1)S(1)} collective-permute-done((bf16[16,768]{1,0:T(8,128)(2,1)S(1)}, bf16[16,768]{1,0:T(8,128)(2,1)S(1)}, u32[]{:S(2)}, u32[]{:S(2)}) %collective-permute-start.1) | collective-permute-done | bytes 24608 | tf_op jit(solution)/shard_map/ppermute | solution.py:243
  47.8 1.4 %outer.1 = f32[64,24,128]{2,1,0:T(8,128)} custom-call(s32[1]{0:T(128)} %bitcast.sub_ref, s32[1]{0:T(128)} %bitcast.1.base_ref, s32[4,64]{1,0:T(4,128)S(1)} %bitcast.12, bf16[80,768]{1,0:T(8,128)(2,1)S(1)} %get-tuple-element.16.mine_ref, bf16[80,768]{1,0:T(8,128)(2,1)S(1)} %collective-permute-done.peer_ref, ...), custom_call_target="tpu_custom_call", output_to_operand_aliasing={{}: (8, {})} | custom-call | tf_op jit(solution)/shard_map/outer/pallas_call | solution.py:269
  (1 shorter events, 0.0 us)
Async XLA Ops:
  2.7 34.0 %all-to-all-start = ((bf16[128,7,2,128]{3,2,1,0:T(2,128)(2,1)}), bf16[128,7,2,128]{3,2,1,0:T(2,128)(2,1)S(1)}, u32[]{:S(2)}, u32[]{:S(2)}) async-start(bf16[128,7,2,128]{3,2,1,0:T(2,128)(2,1)} %bitcast.13), calls=%async_computation | async-start | bytes 917504 | tf_op jit(solution)/shard_map/all_to_all | solution.py:204
  17.8 23.7 %copy-start = (f32[64,128]{1,0:T(8,128)S(1)}, f32[64,128]{1,0:T(8,128)}, u32[]{:S(2)}) copy-start(f32[64,128]{1,0:T(8,128)} %diag_ref.3) | copy-start | bytes 98308
  17.8 23.7 %copy-start.1 = (s32[64,4]{0,1:T(4,128)S(1)}, s32[64,4]{0,1:T(4,128)}, u32[]{:S(2)}) copy-start(s32[64,4]{0,1:T(4,128)} %param.10) | copy-start | bytes 3076
  37.0 1.4 %collective-permute-start = (bf16[80,768]{1,0:T(8,128)(2,1)S(1)}, bf16[80,768]{1,0:T(8,128)(2,1)S(1)}, u32[]{:S(2)}, u32[]{:S(2)}) collective-permute-start(bf16[80,768]{1,0:T(8,128)(2,1)S(1)} %get-tuple-element.17), channel_id=1, source_target_pairs={{0,1},{1,0},{2,3},{3,2},{4,5},{5,4},{6,7},{7,6},{8,9},{9,8},{10,11... | collective-permute-start | bytes 368648 | tf_op jit(solution)/shard_map/ppermute | solution.py:233
  38.5 9.4 %collective-permute-start.1 = (bf16[16,768]{1,0:T(8,128)(2,1)S(1)}, bf16[16,768]{1,0:T(8,128)(2,1)S(1)}, u32[]{:S(2)}, u32[]{:S(2)}) collective-permute-start(bf16[16,768]{1,0:T(8,128)(2,1)S(1)} %edge.1), channel_id=1, source_target_pairs={{1,2},{2,1},{3,4},{4,3},{5,6},{6,5},{7,8},{8,7},{9,10},{10,9},{11,... | collective-permute-start | bytes 73736 | tf_op jit(solution)/shard_map/ppermute | solution.py:243

commit v3 on v2

--- a/solution.py
+++ b/solution.py
@@ -16,6 +16,14 @@
 PARAMS = pltpu.CompilerParams(vmem_limit_bytes=20 * MIB)
 WIDE = pltpu.CompilerParams(vmem_limit_bytes=60 * MIB)
 MSG_ROWS = 14
+
+
+def partition_of(message):
+    z, x, y = message % 8, message // 8 % 4, message // 32
+    return 127 - (z * 16 + y * 4 + x)
+
+
+ORDER = [partition_of(i) for i in range(128)]
 
 
 def iota(shape, dim):
@@ -46,7 +54,7 @@
     live = iota((1, slots), 1) < count_ref[0]
     owner = jnp.where(live, agg // LANES, -1)
     position = agg % LANES
-    to_dest = owner == iota((n_dom, slots), 0)
+    to_dest = owner == partition_of(iota((n_dom, slots), 0))
     before = onehot(iota((slots, slots), 0) < iota((slots, slots), 1))
     rank = dot(onehot(to_dest), before, ((1,), (0,)))
     first = onehot(to_dest & (rank < 0.5))
@@ -202,7 +210,12 @@
 
     messages, tiles_a = lax.optimization_barrier((messages, tiles_a))
     arrived = lax.all_to_all(
-        messages.reshape(n_dom, MSG_ROWS // 2, 2, width), "dom", split_axis=0, concat_axis=0, tiled=True
+        messages.reshape(n_dom, MSG_ROWS // 2, 2, width),
+        "dom",
+        split_axis=0,
+        concat_axis=0,
+        tiled=True,
+        axis_index_groups=[ORDER],
     ).reshape(msg_shape)
 
     per_step = 16

time: 49.5 us -> 44.6 us (0.901)
  waiting for transfers between devices: 14.8 us -> 5.36 us
  starting transfers between devices: 18.1 us -> 22.5 us
    all_to_all x1, waiting for transfers between devices: 11 us -> 4.03 us  [per_device(): lax.all_to_all(messages.reshape(n_dom, MSG_ROWS // 2, 2, width), 'dom', s...]
    ppermute x1, starting transfers between devices: 2.94 us -> 5.55 us  [per_device(): edge = lax.ppermute(edge, both, across)]
    ppermute x1, waiting for transfers between devices: 2.45 us -> 0.01 us  [per_device(): edge = lax.ppermute(edge, both, across)]
    all_to_all x1, starting transfers between devices: 15 us -> 16.8 us  [per_device(): lax.all_to_all(messages.reshape(n_dom, MSG_ROWS // 2, 2, width), 'dom', s...]
  transfers between devices with their start and end apart: 3 -> 3, of which waited for: 3 -> 2; matrix products, arithmetic and copies ran while one was open for 0% -> 0% of each run, Pallas kernels for 24% -> 27%
where the time goes in v3:
time: 44.6 us; the launch traced here: 44.2 us
  starting transfers between devices  22.5 us (50%)
  Pallas kernels  15.7 us (35%)
  waiting for transfers between devices  5.36 us (12%)
  between operations  0.76 us (2%)
    all_to_all x1, starting transfers between devices, per_device(): lax.all_to_all(messages.reshape(n_dom, MSG_ROWS // 2, 2, width), 'dom', s...  16.8 us
    pallas_call x1, Pallas kernels, per_device(): pl.pallas_call(turn_kernel, out_shape=jax.ShapeDtypeStruct((rows_dev, nei...  7.9 us
    ppermute x1, starting transfers between devices, per_device(): edge = lax.ppermute(edge, both, across)  5.55 us
    all_to_all x1, waiting for transfers between devices, per_device(): lax.all_to_all(messages.reshape(n_dom, MSG_ROWS // 2, 2, width), 'dom', s...  4.03 us
    pallas_call x1, Pallas kernels, per_device(): pl.pallas_call(inner_kernel, out_shape=[out_shape, jax.ShapeDtypeStruct((...  3.92 us
    pallas_call x1, Pallas kernels, per_device(): pl.pallas_call(pack_kernel, out_shape=jax.ShapeDtypeStruct(msg_shape, BF1...  2.08 us
    pallas_call x1, Pallas kernels, per_device(): pl.pallas_call(outer_kernel, out_shape=out_shape, in_specs=[smem, smem] +...  1.43 us
    ppermute x1, waiting for transfers between devices, per_device(): peer = lax.ppermute(for_peer, both, [(i, i ^ 1) for i in range(n_dev)])  1.32 us
  transfers between devices with their start and end apart: 3, of which 2 were waited for; matrix products, arithmetic and copies ran while one was open for 0% of the time, Pallas kernels for 27%

profile of v3, /device:TPU:32, one launch (start us, length us, event | category | flops | bytes accessed | tf_op | source)
XLA Modules:
  0.0 44.2 jit_solution(17879479945633651584)
XLA Ops:
  0.7 2.1 %pack.1 = bf16[1792,128]{1,0:T(8,128)(2,1)} custom-call(s32[1]{0:T(128)S(6)} %copy.9.count_hbm, s32[1,104]{1,0:T(1,128)} %bitcast.15, f32[6,104,128]{2,1,0:T(8,128)} %bitcast.14), custom_call_target="tpu_custom_call" | custom-call | tf_op jit(solution)/shard_map/pack/pallas_call | solution.py:195
  2.7 16.8 %all-to-all-start = ((bf16[128,7,2,128]{3,2,1,0:T(2,128)(2,1)}), bf16[128,7,2,128]{3,2,1,0:T(2,128)(2,1)S(1)}, u32[]{:S(2)}, u32[]{:S(2)}) async-start(bf16[128,7,2,128]{3,2,1,0:T(2,128)(2,1)} %bitcast.13), calls=%async_computation | async-start | bytes 917504 | tf_op jit(solution)/shard_map/all_to_all | solution.py:212
  19.6 0.0 copy-start
  19.6 0.0 copy-start.1
  19.6 7.9 %turn.1.tiles_hbm = bf16[64,512,128]{2,1,0:T(8,128)(2,1)} custom-call(bf16[64,4,128,128]{3,2,1,0:T(8,128)(2,1)} %tiles_ref), custom_call_target="tpu_custom_call" | custom-call | bytes 16777216 | tf_op jit(solution)/shard_map/turn/pallas_call | solution.py:222
  27.5 4.0 %all-to-all-done = bf16[128,7,2,128]{3,2,1,0:T(2,128)(2,1)S(1)} async-done(((bf16[128,7,2,128]{3,2,1,0:T(2,128)(2,1)}), bf16[128,7,2,128]{3,2,1,0:T(2,128)(2,1)S(1)}, u32[]{:S(2)}, u32[]{:S(2)}) %all-to-all-start) | async-done | bytes 458784 | tf_op jit(solution)/shard_map/all_to_all | solution.py:212
  31.5 0.3 place.1
  31.9 0.1 collective-permute-start
  32.0 1.3 %collective-permute-done.peer_ref = bf16[80,768]{1,0:T(8,128)(2,1)S(1)} collective-permute-done((bf16[80,768]{1,0:T(8,128)(2,1)S(1)}, bf16[80,768]{1,0:T(8,128)(2,1)S(1)}, u32[]{:S(2)}, u32[]{:S(2)}) %collective-permute-start) | collective-permute-done | bytes 122912 | tf_op jit(solution)/shard_map/ppermute | solution.py:246
  33.3 5.6 %collective-permute-start.1 = (bf16[16,768]{1,0:T(8,128)(2,1)S(1)}, bf16[16,768]{1,0:T(8,128)(2,1)S(1)}, u32[]{:S(2)}, u32[]{:S(2)}) collective-permute-start(bf16[16,768]{1,0:T(8,128)(2,1)S(1)} %edge.1), channel_id=1, source_target_pairs={{1,2},{2,1},{3,4},{4,3},{5,6},{6,5},{7,8},{8,7},{9,10},{10,9},{11,... | collective-permute-start | bytes 73736 | tf_op jit(solution)/shard_map/ppermute | solution.py:256
  38.9 0.0 copy-done
  38.9 0.0 copy-done.1
  38.9 3.9 %inner.1 = (f32[64,24,128]{2,1,0:T(8,128)}, bf16[16,512,128]{2,1,0:T(8,128)(2,1)S(1)}) custom-call(s32[1]{0:T(128)} %bitcast.sub_ref, s32[1]{0:T(128)} %bitcast.1.base_ref, s32[4,64]{1,0:T(4,128)S(1)} %bitcast.11, bf16[80,768]{1,0:T(8,128)(2,1)S(1)} %get-tuple-element.16.mine_ref, bf16[80,768]{1,0:T(8,128)(2,1)S(1)} %collective-permute-done.peer_ref, ...), custom_call_target="tpu_custom_call" | custom-call | flops 150994944 | bytes 8388608 | tf_op jit(solution)/shard_map/inner/pallas_call | solution.py:264
  42.8 0.0 collective-permute-done.1.edge_ref
  42.8 1.4 %outer.1 = f32[64,24,128]{2,1,0:T(8,128)} custom-call(s32[1]{0:T(128)} %bitcast.sub_ref, s32[1]{0:T(128)} %bitcast.1.base_ref, s32[4,64]{1,0:T(4,128)S(1)} %bitcast.12, bf16[80,768]{1,0:T(8,128)(2,1)S(1)} %get-tuple-element.16.mine_ref, bf16[80,768]{1,0:T(8,128)(2,1)S(1)} %collective-permute-done.peer_ref, ...), custom_call_target="tpu_custom_call", output_to_operand_aliasing={{}: (8, {})} | custom-call | tf_op jit(solution)/shard_map/outer/pallas_call | solution.py:282
  (1 shorter events, 0.0 us)
Async XLA Ops:
  2.7 28.8 %all-to-all-start = ((bf16[128,7,2,128]{3,2,1,0:T(2,128)(2,1)}), bf16[128,7,2,128]{3,2,1,0:T(2,128)(2,1)S(1)}, u32[]{:S(2)}, u32[]{:S(2)}) async-start(bf16[128,7,2,128]{3,2,1,0:T(2,128)(2,1)} %bitcast.13), calls=%async_computation | async-start | bytes 917504 | tf_op jit(solution)/shard_map/all_to_all | solution.py:212
  19.6 19.3 %copy-start = (f32[64,128]{1,0:T(8,128)S(1)}, f32[64,128]{1,0:T(8,128)}, u32[]{:S(2)}) copy-start(f32[64,128]{1,0:T(8,128)} %diag_ref.3) | copy-start | bytes 98308
  19.6 19.3 %copy-start.1 = (s32[64,4]{0,1:T(4,128)S(1)}, s32[64,4]{0,1:T(4,128)}, u32[]{:S(2)}) copy-start(s32[64,4]{0,1:T(4,128)} %param.10) | copy-start | bytes 3076
  31.9 1.4 %collective-permute-start = (bf16[80,768]{1,0:T(8,128)(2,1)S(1)}, bf16[80,768]{1,0:T(8,128)(2,1)S(1)}, u32[]{:S(2)}, u32[]{:S(2)}) collective-permute-start(bf16[80,768]{1,0:T(8,128)(2,1)S(1)} %get-tuple-element.17), channel_id=1, source_target_pairs={{0,1},{1,0},{2,3},{3,2},{4,5},{5,4},{6,7},{7,6},{8,9},{9,8},{10,11... | collective-permute-start | bytes 368648 | tf_op jit(solution)/shard_map/ppermute | solution.py:246
  33.3 9.5 %collective-permute-start.1 = (bf16[16,768]{1,0:T(8,128)(2,1)S(1)}, bf16[16,768]{1,0:T(8,128)(2,1)S(1)}, u32[]{:S(2)}, u32[]{:S(2)}) collective-permute-start(bf16[16,768]{1,0:T(8,128)(2,1)S(1)} %edge.1), channel_id=1, source_target_pairs={{1,2},{2,1},{3,4},{4,3},{5,6},{6,5},{7,8},{8,7},{9,10},{10,9},{11,... | collective-permute-start | bytes 73736 | tf_op jit(solution)/shard_map/ppermute | solution.py:256

commit v4 on v3

--- a/solution.py
+++ b/solution.py
@@ -14,7 +14,9 @@
 LANES = 128
 MIB = 2**20
 PARAMS = pltpu.CompilerParams(vmem_limit_bytes=20 * MIB)
+MIDDLE = pltpu.CompilerParams(vmem_limit_bytes=48 * MIB)
 WIDE = pltpu.CompilerParams(vmem_limit_bytes=60 * MIB)
+PARTS = ((0, 24), (24, 48))
 MSG_ROWS = 14
 
 
@@ -100,11 +102,16 @@
     edge_ref[...] = mine_ref[pl.ds(low, halo), :] + peer_ref[pl.ds(low, halo), :]
 
 
-def turn_kernel(tiles_ref, out_ref):
+def turn_kernel(sub_ref, tiles_ref, out_ref, rest_ref):
+    step = pl.program_id(0)
     n_tile, neigh, width, _ = tiles_ref.shape
     for n in range(n_tile):
         for k in range(neigh):
             out_ref[n, k * width : (k + 1) * width, :] = tiles_ref[n, k].T
+
+    @pl.when(step == sub_ref[0] * (pl.num_programs(0) - 1))
+    def _():
+        rest_ref[...] = out_ref[...]
 
 
 def gather(ext, local, left, neigh, modes):
@@ -116,8 +123,8 @@
             left[pl.ds(c * neigh + k, total, stride=modes * neigh), :] = got[:, c * LANES : (c + 1) * LANES]
 
 
-def smooth_row(t, left, tiles, diag_ref, neigh, rows):
-    lhs = left[pl.ds(pl.multiple_of(t * rows, 8), rows), :]
+def smooth_row(n, t, left, tiles, diag_ref, neigh, rows):
+    lhs = left[n * rows : (n + 1) * rows, :]
     row_k = iota((rows, LANES), 0) % neigh
     spread = jnp.concatenate([jnp.where(row_k == k, lhs, 0.0).astype(BF16) for k in range(neigh)], axis=1)
     product = dot(spread, tiles, ((1,), (0,)))
@@ -126,54 +133,39 @@
 
 
 def inner_kernel(
-    sub_ref, base_ref, cols_ref, mine_ref, peer_ref, diag_ref, tiles_hbm, out_hbm, rest_ref, left, tiles, done, in_sems, out_sems
+    sub_ref, base_ref, cols_ref, mine_ref, peer_ref, diag_ref, tiles_hbm, done_ref, left, tiles, sems
 ):
-    count, rows, _ = done.shape
-    neigh, total = cols_ref.shape
-    rest = total - count
-    modes = rows // neigh
-    chunk = count // (in_sems.shape[0] - 1)
-    sub = sub_ref[0]
-    start = (1 - sub) * rest
-
+    count, rows, _ = done_ref.shape
+    neigh = cols_ref.shape[0]
+    start = (1 - sub_ref[0]) * (tiles_hbm.shape[0] - count)
     fetches = []
-    for i in range(count // chunk):
-        place = pl.ds(i * chunk, chunk)
-        fetches.append(pltpu.make_async_copy(tiles_hbm.at[pl.ds(start + i * chunk, chunk)], tiles.at[place], in_sems.at[i]))
-    fetches.append(pltpu.make_async_copy(tiles_hbm.at[pl.ds(sub * count, rest)], rest_ref, in_sems.at[count // chunk]))
-    for fetch in fetches:
-        fetch.start()
-
-    gather(mine_ref[...] + peer_ref[...], cols_ref[...] - base_ref[0], left, neigh, modes)
-
-    writes = []
-    for i in range(count // chunk):
-        fetches[i].wait()
-        for n in range(i * chunk, (i + 1) * chunk):
-            done[n] = smooth_row(start + n, left, tiles[n], diag_ref, neigh, rows)
-        place = pl.ds(i * chunk, chunk)
-        writes.append(pltpu.make_async_copy(done.at[place], out_hbm.at[pl.ds(start + i * chunk, chunk)], out_sems.at[i]))
-        writes[-1].start()
-    fetches[-1].wait()
-    for write in writes:
-        write.wait()
+    for i, (low, high) in enumerate(PARTS):
+        there, here = pl.ds(start + low, high - low), pl.ds(low, high - low)
+        fetches.append(pltpu.make_async_copy(tiles_hbm.at[there], tiles.at[here], sems.at[i]))
+        fetches[-1].start()
+    gather(mine_ref[...] + peer_ref[...], cols_ref[...] - base_ref[0], left, neigh, rows // neigh)
+    for fetch, (low, high) in zip(fetches, PARTS):
+        fetch.wait()
+        for n in range(low, high):
+            done_ref[n] = smooth_row(n, start + n, left, tiles[n], diag_ref, neigh, rows)
 
 
 def outer_kernel(
-    sub_ref, base_ref, cols_ref, mine_ref, peer_ref, edge_ref, diag_ref, rest_ref, begun_hbm, out_hbm, left, done, sem
+    sub_ref, base_ref, cols_ref, mine_ref, peer_ref, edge_ref, diag_ref, rest_ref, inner_ref, out_hbm, left, done, sems
 ):
-    del begun_hbm
-    rest, rows, _ = done.shape
-    neigh, total = cols_ref.shape
-    modes = rows // neigh
-    start = sub_ref[0] * (total - rest)
+    count, rest = inner_ref.shape[0], done.shape[0]
+    rows, neigh = done.shape[1], cols_ref.shape[0]
+    write_inner = pltpu.make_async_copy(inner_ref, out_hbm.at[pl.ds((1 - sub_ref[0]) * rest, count)], sems.at[0])
+    write_inner.start()
+    start = sub_ref[0] * count
     ext = jnp.concatenate([mine_ref[...] + peer_ref[...], edge_ref[...]], axis=0)
     local = cols_ref[...] - base_ref[0]
-    gather(ext, jnp.where(local < 0, local + ext.shape[0], local), left, neigh, modes)
+    gather(ext, jnp.where(local < 0, local + ext.shape[0], local), left, neigh, rows // neigh)
     for n in range(rest):
-        done[n] = smooth_row(start + n, left, rest_ref[n], diag_ref, neigh, rows)
-    write = pltpu.make_async_copy(done, out_hbm.at[pl.ds(start, rest)], sem)
+        done[n] = smooth_row(n, start + n, left, rest_ref[n], diag_ref, neigh, rows)
+    write = pltpu.make_async_copy(done, out_hbm.at[pl.ds(start, rest)], sems.at[1])
     write.start()
+    write_inner.wait()
     write.wait()
 
 
@@ -218,18 +210,25 @@
         axis_index_groups=[ORDER],
     ).reshape(msg_shape)
 
-    per_step = 16
-    turned = pl.pallas_call(
+    turned, rest = pl.pallas_call(
         turn_kernel,
-        out_shape=jax.ShapeDtypeStruct((rows_dev, neigh * width, width), BF16),
-        grid=(rows_dev // per_step,),
-        in_specs=[pl.BlockSpec((per_step, neigh, width, width), lambda i: (i, 0, 0, 0))],
-        out_specs=pl.BlockSpec((per_step, neigh * width, width), lambda i: (i, 0, 0)),
+        out_shape=[jax.ShapeDtypeStruct((n, neigh * width, width), BF16) for n in (rows_dev, halo)],
+        grid=(rows_dev // halo,),
+        in_specs=[smem, pl.BlockSpec((halo, neigh, width, width), lambda i: (i, 0, 0, 0))],
+        out_specs=[
+            pl.BlockSpec((halo, neigh * width, width), lambda i: (i, 0, 0)),
+            pl.BlockSpec((halo, neigh * width, width), lambda i: (0, 0, 0)),
+        ],
         compiler_params=WIDE,
         cost_estimate=pl.CostEstimate(flops=0, bytes_accessed=2 * tiles_a.size * 2, transcendentals=0),
         name="turn",
-    )(tiles_a)
-    arrived, turned = lax.optimization_barrier((arrived, turned))
+    )(sub.reshape(1), tiles_a)
+    inner = rows_dev - halo
+    inner_cols = lax.dynamic_slice_in_dim(tile_cols, (1 - sub) * halo, inner, 0).T
+    outer_cols = lax.dynamic_slice_in_dim(tile_cols, sub * inner, halo, 0).T
+    arrived, turned, rest, inner_cols, outer_cols = lax.optimization_barrier(
+        (arrived, turned, rest, inner_cols, outer_cols)
+    )
 
     mine, for_peer = pl.pallas_call(
         place_kernel,
@@ -257,38 +256,35 @@
 
     base = device * rows_dev - sub * halo
     rows = modes * neigh
-    inner = rows_dev - halo
-    chunk = 8
-    out_shape = jax.ShapeDtypeStruct((rows_dev, rows, width), F32)
-    left_shape = VMEM((rows_dev * rows, width), F32)
-    begun, rest = pl.pallas_call(
+    inner_out = pl.pallas_call(
         inner_kernel,
-        out_shape=[out_shape, jax.ShapeDtypeStruct((halo, neigh * width, width), BF16)],
+        out_shape=jax.ShapeDtypeStruct((inner, rows, width), F32),
         in_specs=[smem, smem] + [vmem] * 4 + [hbm],
-        out_specs=[hbm, vmem],
+        out_specs=vmem,
         scratch_shapes=[
-            left_shape,
+            VMEM((inner * rows, width), F32),
             VMEM((inner, neigh * width, width), BF16),
-            VMEM((inner, rows, width), F32),
-            pltpu.SemaphoreType.DMA((inner // chunk + 1,)),
-            pltpu.SemaphoreType.DMA((inner // chunk,)),
+            pltpu.SemaphoreType.DMA((len(PARTS),)),
         ],
-        compiler_params=pltpu.CompilerParams(vmem_limit_bytes=48 * MIB),
+        compiler_params=MIDDLE,
         cost_estimate=pl.CostEstimate(
             flops=2 * inner * rows * neigh * width * width, bytes_accessed=tiles_a.size * 2, transcendentals=0
         ),
         name="inner",
-    )(sub.reshape(1), base.reshape(1), tile_cols.T, mine, peer, inv_diag, turned)
+    )(sub.reshape(1), base.reshape(1), inner_cols, mine, peer, inv_diag, turned)
     out = pl.pallas_call(
         outer_kernel,
-        out_shape=out_shape,
-        in_specs=[smem, smem] + [vmem] * 6 + [hbm],
+        out_shape=jax.ShapeDtypeStruct((rows_dev, rows, width), F32),
+        in_specs=[smem, smem] + [vmem] * 7,
         out_specs=hbm,
-        scratch_shapes=[left_shape, VMEM((halo, rows, width), F32), pltpu.SemaphoreType.DMA],
-        input_output_aliases={8: 0},
+        scratch_shapes=[
+            VMEM((halo * rows, width), F32),
+            VMEM((halo, rows, width), F32),
+            pltpu.SemaphoreType.DMA((2,)),
+        ],
         compiler_params=PARAMS,
         name="outer",
-    )(sub.reshape(1), base.reshape(1), tile_cols.T, mine, peer, edge, inv_diag, rest, begun)
+    )(sub.reshape(1), base.reshape(1), outer_cols, mine, peer, edge, inv_diag, rest, inner_out)
     return jnp.transpose(out.reshape(rows_dev, modes, neigh, width), (0, 2, 1, 3))
 
 

time: 44.6 us -> 44.3 us (level)
  waiting for transfers between devices: 5.36 us -> 4.76 us
    all_to_all x1, waiting for transfers between devices: 4.03 us -> 3.1 us  [per_device(): lax.all_to_all(messages.reshape(n_dom, MSG_ROWS // 2, 2, width), 'dom', s...]
  transfers between devices with their start and end apart: 3 -> 3, of which waited for: 2 -> 3; matrix products, arithmetic and copies ran while one was open for 0% -> 0% of each run, Pallas kernels for 27% -> 28%
where the time goes in v4:
time: 44.3 us; the launch traced here: 44 us
  starting transfers between devices  22.5 us (51%)
  Pallas kernels  15.9 us (36%)
  waiting for transfers between devices  4.76 us (11%)
  between operations  0.75 us (2%)
    all_to_all x1, starting transfers between devices, per_device(): lax.all_to_all(messages.reshape(n_dom, MSG_ROWS // 2, 2, width), 'dom', s...  16.8 us
    pallas_call x1, Pallas kernels, per_device(): pl.pallas_call(turn_kernel, out_shape=[jax.ShapeDtypeStruct((n, neigh * w...  8.69 us
    ppermute x1, starting transfers between devices, per_device(): edge = lax.ppermute(edge, both, across)  5.55 us
    pallas_call x1, Pallas kernels, per_device(): pl.pallas_call(inner_kernel, out_shape=jax.ShapeDtypeStruct((inner, rows,...  3.42 us
    all_to_all x1, waiting for transfers between devices, per_device(): lax.all_to_all(messages.reshape(n_dom, MSG_ROWS // 2, 2, width), 'dom', s...  3.1 us
    pallas_call x1, Pallas kernels, per_device(): pl.pallas_call(pack_kernel, out_shape=jax.ShapeDtypeStruct(msg_shape, BF1...  2.08 us
    pallas_call x1, Pallas kernels, per_device(): pl.pallas_call(outer_kernel, out_shape=jax.ShapeDtypeStruct((rows_dev, ro...  1.36 us
    ppermute x1, waiting for transfers between devices, per_device(): peer = lax.ppermute(for_peer, both, [(i, i ^ 1) for i in range(n_dev)])  1.32 us
  transfers between devices with their start and end apart: 3, of which 3 were waited for; matrix products, arithmetic and copies ran while one was open for 0% of the time, Pallas kernels for 28%

profile of v4, /device:TPU:32, one launch (start us, length us, event | category | flops | bytes accessed | tf_op | source)
XLA Modules:
  0.0 44.0 jit_solution(6353965882475699046)
XLA Ops:
  0.0 0.0 copy-start
  0.0 0.0 copy-start.2
  0.7 2.1 %pack.1 = bf16[1792,128]{1,0:T(8,128)(2,1)} custom-call(s32[1]{0:T(128)S(6)} %copy.7.count_hbm, s32[1,104]{1,0:T(1,128)} %bitcast.16, f32[6,104,128]{2,1,0:T(8,128)} %bitcast.15), custom_call_target="tpu_custom_call" | custom-call | tf_op jit(solution)/shard_map/pack/pallas_call | solution.py:187
  2.8 16.8 %all-to-all-start = ((bf16[128,7,2,128]{3,2,1,0:T(2,128)(2,1)}), bf16[128,7,2,128]{3,2,1,0:T(2,128)(2,1)S(1)}, u32[]{:S(2)}, u32[]{:S(2)}) async-start(bf16[128,7,2,128]{3,2,1,0:T(2,128)(2,1)} %bitcast.14), calls=%async_computation | async-start | bytes 917504 | tf_op jit(solution)/shard_map/all_to_all | solution.py:204
  19.6 8.7 %turn.1 = (bf16[64,512,128]{2,1,0:T(8,128)(2,1)}, bf16[16,512,128]{2,1,0:T(8,128)(2,1)}) custom-call(s32[1]{0:T(128)} %bitcast.sub_ref, bf16[64,4,128,128]{3,2,1,0:T(8,128)(2,1)} %tiles_ref), custom_call_target="tpu_custom_call" | custom-call | bytes 16777216 | tf_op jit(solution)/shard_map/turn/pallas_call | solution.py:213
  28.3 0.0 copy-done
  28.3 0.0 copy-start.1
  28.3 0.1 dynamic-slice_bitcast_fusion.cols_ref
  28.4 0.1 dynamic-slice_bitcast_fusion.1.cols_ref
  28.5 3.1 %all-to-all-done = bf16[128,7,2,128]{3,2,1,0:T(2,128)(2,1)S(1)} async-done(((bf16[128,7,2,128]{3,2,1,0:T(2,128)(2,1)}), bf16[128,7,2,128]{3,2,1,0:T(2,128)(2,1)S(1)}, u32[]{:S(2)}, u32[]{:S(2)}) %all-to-all-start) | async-done | bytes 458784 | tf_op jit(solution)/shard_map/all_to_all | solution.py:204
  31.6 0.3 place.1
  31.9 0.1 collective-permute-start
  32.0 1.3 %collective-permute-done.peer_ref = bf16[80,768]{1,0:T(8,128)(2,1)S(1)} collective-permute-done((bf16[80,768]{1,0:T(8,128)(2,1)S(1)}, bf16[80,768]{1,0:T(8,128)(2,1)S(1)}, u32[]{:S(2)}, u32[]{:S(2)}) %collective-permute-start) | collective-permute-done | bytes 122912 | tf_op jit(solution)/shard_map/ppermute | solution.py:245
  33.3 5.6 %collective-permute-start.1 = (bf16[16,768]{1,0:T(8,128)(2,1)S(1)}, bf16[16,768]{1,0:T(8,128)(2,1)S(1)}, u32[]{:S(2)}, u32[]{:S(2)}) collective-permute-start(bf16[16,768]{1,0:T(8,128)(2,1)S(1)} %edge.1), channel_id=1, source_target_pairs={{1,2},{2,1},{3,4},{4,3},{5,6},{6,5},{7,8},{8,7},{9,10},{10,9},{11,... | collective-permute-start | bytes 73736 | tf_op jit(solution)/shard_map/ppermute | solution.py:255
  38.9 0.0 copy-done.2
  38.9 3.4 %inner.1.inner_ref = f32[48,24,128]{2,1,0:T(8,128)S(1)} custom-call(s32[1]{0:T(128)} %bitcast.sub_ref, s32[1]{0:T(128)} %bitcast.1.base_ref, s32[4,48]{1,0:T(4,128)S(1)} %dynamic-slice_bitcast_fusion.1.cols_ref, bf16[80,768]{1,0:T(8,128)(2,1)S(1)} %get-tuple-element.22.mine_ref, bf16[80,768]{1,0:T(8,128)(2,1)S(1)} %collective-permute-done.peer_ref, ...), custom_call_target="tpu_custom_call" | custom-call | flops 150994944 | bytes 8388608 | tf_op jit(solution)/shard_map/inner/pallas_call | solution.py:259
  42.3 0.3 collective-permute-done.1.edge_ref
  42.7 0.0 copy-done.1
  42.7 1.4 %outer.1 = f32[64,24,128]{2,1,0:T(8,128)} custom-call(s32[1]{0:T(128)} %bitcast.sub_ref, s32[1]{0:T(128)} %bitcast.1.base_ref, s32[4,16]{1,0:T(4,128)S(1)} %dynamic-slice_bitcast_fusion.cols_ref, bf16[80,768]{1,0:T(8,128)(2,1)S(1)} %get-tuple-element.22.mine_ref, bf16[80,768]{1,0:T(8,128)(2,1)S(1)} %collective-permute-done.peer_ref, ...), custom_call_target="tpu_custom_call" | custom-call | tf_op jit(solution)/shard_map/outer/pallas_call | solution.py:275
  (1 shorter events, 0.0 us)
Async XLA Ops:
  0.0 28.3 %copy-start = (s32[64,4]{0,1:T(4,128)S(1)}, s32[64,4]{0,1:T(4,128)}, u32[]{:S(2)}) copy-start(s32[64,4]{0,1:T(4,128)} %param.10) | copy-start | bytes 3076
  0.0 38.9 %copy-start.2 = (f32[64,128]{1,0:T(8,128)S(1)}, f32[64,128]{1,0:T(8,128)}, u32[]{:S(2)}) copy-start(f32[64,128]{1,0:T(8,128)} %diag_ref.3) | copy-start | bytes 98308
  2.8 28.8 %all-to-all-start = ((bf16[128,7,2,128]{3,2,1,0:T(2,128)(2,1)}), bf16[128,7,2,128]{3,2,1,0:T(2,128)(2,1)S(1)}, u32[]{:S(2)}, u32[]{:S(2)}) async-start(bf16[128,7,2,128]{3,2,1,0:T(2,128)(2,1)} %bitcast.14), calls=%async_computation | async-start | bytes 917504 | tf_op jit(solution)/shard_map/all_to_all | solution.py:204
  28.3 14.4 %copy-start.1 = (bf16[16,512,128]{2,1,0:T(8,128)(2,1)S(1)}, bf16[16,512,128]{2,1,0:T(8,128)(2,1)}, u32[]{:S(2)}) copy-start(bf16[16,512,128]{2,1,0:T(8,128)(2,1)} %get-tuple-element.24.rest_ref) | copy-start | bytes 6291460
  31.9 1.4 %collective-permute-start = (bf16[80,768]{1,0:T(8,128)(2,1)S(1)}, bf16[80,768]{1,0:T(8,128)(2,1)S(1)}, u32[]{:S(2)}, u32[]{:S(2)}) collective-permute-start(bf16[80,768]{1,0:T(8,128)(2,1)S(1)} %get-tuple-element.23), channel_id=1, source_target_pairs={{0,1},{1,0},{2,3},{3,2},{4,5},{5,4},{6,7},{7,6},{8,9},{9,8},{10,11... | collective-permute-start | bytes 368648 | tf_op jit(solution)/shard_map/ppermute | solution.py:245
  33.3 9.4 %collective-permute-start.1 = (bf16[16,768]{1,0:T(8,128)(2,1)S(1)}, bf16[16,768]{1,0:T(8,128)(2,1)S(1)}, u32[]{:S(2)}, u32[]{:S(2)}) collective-permute-start(bf16[16,768]{1,0:T(8,128)(2,1)S(1)} %edge.1), channel_id=1, source_target_pairs={{1,2},{2,1},{3,4},{4,3},{5,6},{6,5},{7,8},{8,7},{9,10},{10,9},{11,... | collective-permute-start | bytes 73736 | tf_op jit(solution)/shard_map/ppermute | solution.py:255
